TPU v7x, 32 devices: a whole 2x2x4 slice. The times are simulated.
32 devices in a mesh: rows: 8 (over z, x), cols: 4 (over y, core).
Axes of the slice: x: 2, y: 2, z: 4, core: 2. Of those that a mesh axis runs over, the one named last changes fastest.
Arguments:
- capsule_points: float32 [3, 16384], P(None, 'rows'), may hold values from 0 to 1
- capsule_weight: float32 [16384], P('rows'), may hold values from 0.3 to 9
- wall_points: float32 [3, 8192], P(None, 'cols'), may hold values from 0 to 1
- wall_weight: float32 [8192], P('cols'), may hold values from 0.3 to 3
- gauss_sketch: bfloat16 [8192, 512], P('cols'), may hold values from -0.0625 to 0.0625
- far_pairs: int32 [8, 4, 48, 2], P('rows', 'cols'), may hold values from -1 to 63, as said below
- tile_count: int32 [8, 4], P('rows', 'cols'), may hold values from 16 to 48, as said below
Outputs:
- basis_out: bfloat16 [16384, 512], P(('rows', 'cols'))
- projected: float32 [512, 8192], P('rows', 'cols')
Inputs may be any that keep to these rules, and one draw needn't show every extreme that they name: For every p and q the first tile_count[p, q] entries of far_pairs[p, q] are distinct pairs whose row block lies in p * 8 to (p + 1) * 8 - 1 and whose column block lies in q * 8 to (q + 1) * 8 - 1; the later entries are -1 and name no tile. `tile_count`: some device has exactly 48 far tiles in every draw.
All inputs are finite; a program needn't handle non-finite values.
Results may differ from a plain program's by a relative error of at most 0.0052.
Values may be sent and summed in bfloat16 or wider, within the bound.
A program may use at most 128 MiB of HBM per device.

v0:
```python
import math

import jax
import jax.numpy as jnp
from jax import lax
from jax.sharding import PartitionSpec as P

TILE = 256


WAVENUMBER = 150.0
WALL_GAP = 2.0
HIGHEST = lax.Precision.HIGHEST


def partner(value, axis, bit):
    mask = 2**bit
    pairs = [(source, source ^ mask) for source in range(lax.axis_size(axis))]
    return lax.ppermute(value, axis, pairs)


def kernel_tile(row_points, row_weight, col_points, col_weight):
    diff_x = row_points[0][:, None] - col_points[0][None, :]
    diff_y = row_points[1][:, None] - col_points[1][None, :]
    diff_z = row_points[2][:, None] - col_points[2][None, :] - WALL_GAP
    distance = jnp.sqrt(diff_x * diff_x + diff_y * diff_y + diff_z * diff_z)
    return (
        row_weight[:, None] * col_weight[None, :] * jnp.cos(WAVENUMBER * distance) / distance
    ).astype(jnp.bfloat16)


def cut_block(points, weights, block_index, tile_width):
    first_cell = block_index * tile_width
    return (
        lax.dynamic_slice_in_dim(points, first_cell, tile_width, 1),
        lax.dynamic_slice_in_dim(weights, first_cell, tile_width, 0),
    )


def fill_cache(
    cache_tiles,
    row_points,
    row_weight,
    wall_points,
    wall_weight,
    rows_list,
    cols_list,
    list_offset,
    slot_stop,
    tile_width,
):

    def cache_step(slot_index, cached):
        list_entry = list_offset + slot_index
        row_pts, row_wts = cut_block(row_points, row_weight, rows_list[list_entry], tile_width)
        col_pts, col_wts = cut_block(wall_points, wall_weight, cols_list[list_entry], tile_width)
        fresh_tile = kernel_tile(row_pts, row_wts, col_pts, col_wts)
        return lax.dynamic_update_slice_in_dim(cached, fresh_tile[None], slot_index, 0)

    return lax.fori_loop(0, slot_stop, cache_step, cache_tiles)


def sketch_partial(
    cache_tiles, gauss_sketch, rows_list, cols_list, slot_stop, local_rows, tile_width
):

    def sketch_step(slot_index, running):
        col_first = cols_list[slot_index] * tile_width
        sketch_part = lax.dynamic_slice_in_dim(gauss_sketch, col_first, tile_width, 0)
        product = jnp.dot(cache_tiles[slot_index], sketch_part, preferred_element_type=jnp.float32)
        row_first = rows_list[slot_index] * tile_width
        current = lax.dynamic_slice_in_dim(running, row_first, tile_width, 0)
        return lax.dynamic_update_slice_in_dim(running, current + product, row_first, 0)

    return lax.fori_loop(
        0, slot_stop, sketch_step, jnp.zeros((local_rows, gauss_sketch.shape[1]), jnp.float32)
    )


def add_products(
    running,
    basis_rows,
    cache_tiles,
    rows_list,
    cols_list,
    list_offset,
    slot_stop,
    row_start,
    row_count,
    tile_width,
):

    def product_step(slot_index, partial_value):
        list_entry = list_offset + slot_index
        basis_part = lax.dynamic_slice(
            basis_rows, (rows_list[list_entry] * tile_width, row_start), (tile_width, row_count)
        )
        product = lax.dot_general(
            basis_part,
            cache_tiles[slot_index],
            (((0,), (0,)), ((), ())),
            preferred_element_type=jnp.float32,
        )
        col_first = cols_list[list_entry] * tile_width
        current = lax.dynamic_slice_in_dim(partial_value, col_first, tile_width, 1)
        return lax.dynamic_update_slice_in_dim(partial_value, current + product, col_first, 1)

    return lax.fori_loop(0, slot_stop, product_step, running)


def gram_local(sketch_rows):
    return lax.dot_general(
        sketch_rows,
        sketch_rows,
        (((0,), (0,)), ((), ())),
        precision=HIGHEST,
        preferred_element_type=jnp.float32,
    )


def basis_map(gram_total, identity):
    lower = jnp.linalg.cholesky(gram_total)
    inverse = jax.scipy.linalg.solve_triangular(lower, identity, lower=True)
    return inverse.T


def per_device(
    capsule_points, capsule_weight, wall_points, wall_weight, gauss_sketch, far_pairs, tile_count
):
    tile_width = TILE
    row_dev = lax.axis_index("rows")
    col_dev = lax.axis_index("cols")
    local_rows = capsule_points.shape[1]
    wall_cells = wall_points.shape[1]
    row_blocks = local_rows // tile_width
    col_blocks = wall_cells // tile_width
    samples = gauss_sketch.shape[1]
    slot_total = far_pairs.shape[2]
    own_list = far_pairs[0, 0]
    own_count = tile_count[0, 0]
    own_rows = own_list[:, 0] - row_dev * row_blocks
    own_cols = own_list[:, 1] - col_dev * col_blocks
    own_cache = fill_cache(
        jnp.zeros((slot_total, tile_width, tile_width), jnp.bfloat16),
        capsule_points,
        capsule_weight,
        wall_points,
        wall_weight,
        own_rows,
        own_cols,
        0,
        own_count,
        tile_width,
    )
    partial_y = sketch_partial(
        own_cache, gauss_sketch, own_rows, own_cols, own_count, local_rows, tile_width
    )
    identity = jnp.eye(samples, dtype=jnp.float32)
    basis_scale = math.sqrt(local_rows * lax.axis_size("rows"))
    whole_y = lax.psum(partial_y, "cols")
    gram_total = lax.psum(gram_local(whole_y), "rows")
    whole_q = jnp.dot(
        whole_y,
        basis_map(gram_total, identity),
        precision=HIGHEST,
        preferred_element_type=jnp.float32,
    )
    share_rows = local_rows // lax.axis_size("cols")
    basis_out = (
        basis_scale * lax.dynamic_slice_in_dim(whole_q, col_dev * share_rows, share_rows, 0)
    ).astype(jnp.bfloat16)
    q_round = whole_q.astype(jnp.bfloat16)
    partner_list, partner_count = partner((own_list, own_count), "rows", 0)
    partner_points, partner_weight = partner((capsule_points, capsule_weight), "rows", 0)
    partner_basis = partner(q_round, "rows", 0)
    partner_dev = jnp.bitwise_xor(row_dev, 1)
    give_away = jnp.maximum(own_count - partner_count, 0) // 2
    take_over = jnp.maximum(partner_count - own_count, 0) // 2
    partner_rows = partner_list[:, 0] - partner_dev * row_blocks
    partner_cols = partner_list[:, 1] - col_dev * col_blocks
    partner_first = partner_count - take_over
    partner_cache = fill_cache(
        jnp.zeros((slot_total // 2 + 1, tile_width, tile_width), jnp.bfloat16),
        partner_points,
        partner_weight,
        wall_points,
        wall_weight,
        partner_rows,
        partner_cols,
        partner_first,
        take_over,
        tile_width,
    )
    own_stop = own_count - give_away
    row_start = jnp.int32(0)
    running = jnp.zeros(
        (samples // lax.axis_size("rows") * lax.axis_size("rows"), wall_cells), jnp.float32
    )
    running = add_products(
        running,
        q_round,
        own_cache,
        own_rows,
        own_cols,
        0,
        own_stop,
        row_start,
        samples // lax.axis_size("rows") * lax.axis_size("rows"),
        tile_width,
    )
    projected = lax.psum_scatter(
        add_products(
            running,
            partner_basis,
            partner_cache,
            partner_rows,
            partner_cols,
            partner_first,
            take_over,
            row_start,
            samples // lax.axis_size("rows") * lax.axis_size("rows"),
            tile_width,
        ),
        "rows",
        scatter_dimension=0,
        tiled=True,
    )
    return (basis_out, projected)


def solution(mesh):
    placed = (
        P(None, "rows"),
        P("rows"),
        P(None, "cols"),
        P("cols"),
        P("cols", None),
        P("rows", "cols", None, None),
        P("rows", "cols"),
    )
    return jax.shard_map(
        per_device,
        mesh=mesh,
        in_specs=placed,
        out_specs=(P(("rows", "cols"), None), P("rows", "cols")),
        check_vma=False,
    )
```

profile of v0, /device:TPU:11, one launch (start us, length us, event | category | flops | bytes accessed | tf_op | source)
XLA Modules:
  0.0 1265.2 jit_solution(13801621759761522595)
XLA Ops:
  8.0 3.4 broadcast_in_dim.14
  11.4 166.1 %while.55 = (s32[]{:T(128)}, bf16[48,256,256]{2,1,0:T(8,128)(2,1)}, s32[]{:T(128)}, s32[48]{0:T(128)S(1)}, f32[2048]{0:T(1024)S(1)}, /*index=5*/s32[48]{0:T(128)...) while((s32[]{:T(128)}, bf16[48,256,256]{2,1,0:T(8,128)(2,1)}, ...), condition=%wide.region_1.0_spmd, body=%wide.region_0.0_spmd.sunk | while | flops 917519 | bytes 156007 | solution.py:60
  177.5 2.6 broadcast_in_dim.13
  180.1 129.8 %while.56 = (s32[]{:T(128)}, f32[2048,512]{1,0:T(8,128)}, s32[]{:T(128)}, s32[48]{0:T(128)S(1)}, bf16[48,256,256]{2,1,0:T(8,128)(2,1)}, /*index=5*/s32[48]{0:T(1...) while((s32[]{:T(128)}, f32[2048,512]{1,0:T(8,128)}, ...), condition=%wide.region_3.0_spmd, body=%wide.region_2.0_spmd.sunk | while | flops 67239952 | bytes 1442079 | solution.py:75
  194.0 2.2 fusion.83
  199.4 2.2 fusion.83
  215.5 2.2 fusion.83
  247.7 2.2 fusion.83
  269.2 2.3 fusion.83
  280.0 2.2 fusion.83
  290.8 2.3 fusion.83
  310.0 379.9 %all-reduce.4.cloned.1.call-done = f32[2048,512]{1,0:T(8,128)} async-done(((f32[2048,512]{1,0:T(8,128)}), f32[2048,512]{1,0:T(8,128)}) %all-reduce.4.cloned.1.call-update) | async-done | bytes 4194320 | tf_op jit(solution)/shard_map/psum | solution.py:160
  689.8 11.4 fusion.59
  708.3 70.4 %all-reduce.6.cloned.1.call-done = f32[512,512]{0,1:T(8,128)} async-done(((f32[512,512]{0,1:T(8,128)}), f32[512,512]{0,1:T(8,128)}) %all-reduce.6.cloned.1.call-update) | async-done | bytes 1048592 | tf_op jit(solution)/shard_map/psum | solution.py:161
  781.7 11.7 cholesky.104
  794.1 9.8 custom-call.31
  804.6 11.7 cholesky.217
  816.8 10.0 custom-call.32
  827.5 11.7 cholesky.238
  839.2 9.8 custom-call.33
  849.7 11.9 cholesky.255
  867.4 10.5 while.60
  878.0 40.1 %custom-call.34 = f32[4,128,128]{1,2,0:T(8,128)S(1)} custom-call(f32[4,128,128]{2,1,0:T(8,128)} %get-tuple-element.377), custom_call_target="InvertDiagBlocksLowerTriangular" | custom-call | tf_op jit(solution)/shard_map/jit(_solve_triangular)/triangular_solve | solution.py:123
  922.1 8.6 fusion.58
  931.9 2.6 broadcast_in_dim.22
  934.5 100.5 %while.57 = (s32[]{:T(128)}, f32[512,2048]{1,0:T(8,128)}, s32[]{:T(128)}, s32[48]{0:T(128)S(1)}, s32[48]{0:T(128)S(1)}, /*index=5*/bf16[2048,512]{1,0:T(8,128)(2...) while((s32[]{:T(128)}, f32[512,2048]{1,0:T(8,128)}, ...), condition=%wide.region_15.16_spmd, body=%wide.region_14.15_spmd.sunk | while | flops 67239952 | bytes 1442079 | solution.py:108
  937.0 2.3 fusion.86
  941.8 2.3 fusion.86
  946.5 2.3 fusion.86
  951.3 2.3 fusion.86
  956.1 2.3 fusion.86
  960.9 2.3 fusion.86
  965.7 2.3 fusion.86
  970.5 2.3 fusion.86
  975.3 2.3 fusion.86
  980.0 2.3 fusion.86
  984.8 2.3 fusion.86
  989.6 2.3 fusion.86
  994.4 2.3 fusion.86
  999.2 2.3 fusion.86
  1004.0 2.3 fusion.86
  1008.8 2.3 fusion.86
  1013.6 2.3 fusion.86
  1018.4 2.3 fusion.86
  1023.2 2.3 fusion.86
  1027.9 2.3 fusion.86
  1032.7 2.3 fusion.86
  1037.2 221.0 %reduce-scatter.2.cloned.1.call-done = f32[64,2048]{1,0:T(8,128)} async-done(((f32[512,2048]{1,0:T(8,128)}), f32[64,2048]{1,0:T(8,128)}) %reduce-scatter.2.cloned.1.call-update) | async-done | bytes 524304 | tf_op jit(solution)/shard_map/reduce_scatter | solution.py:211
  (331 shorter events, 241.6 us)
Async XLA Ops:
  7.2 4.2 copy-start.2
  7.2 4.2 copy-start.1
  7.2 682.7 %all-reduce.4.cloned.1.call-start = ((), (), s32[]{:S(2)}) async-start(), calls=%async_computation.1 | async-start | bytes 8388608 | tf_op jit(solution)/shard_map/psum | solution.py:160
  309.9 391.4 %copy-start.3 = (s32[48]{0:T(128)}, s32[48]{0:T(128)S(1)}, u32[]{:S(2)}) copy-start(s32[48]{0:T(128)S(1)} %get-tuple-element.1070) | copy-start | bytes 580
  309.9 391.4 %copy-start.5 = (s32[48]{0:T(128)}, s32[48]{0:T(128)S(1)}, u32[]{:S(2)}) copy-start(s32[48]{0:T(128)S(1)} %get-tuple-element.1072) | copy-start | bytes 580
  309.9 468.8 %all-reduce.6.cloned.1.call-start = ((), (), s32[]{:S(2)}) async-start(), calls=%async_computation.2 | async-start | bytes 2097152 | tf_op jit(solution)/shard_map/psum | solution.py:161
  701.3 556.9 %reduce-scatter.2.cloned.1.call-start = ((), (), s32[]{:S(2)}) async-start(), calls=%async_computation.3 | async-start | bytes 4718592 | tf_op jit(solution)/shard_map/reduce_scatter | solution.py:211
  701.5 5.1 collective-permute-start
  701.9 228.8 %collective-permute-start.1 = (s32[48,2]{0,1:T(2,128)}, s32[48,2]{0,1:T(2,128)}, u32[]{:S(2)}, u32[]{:S(2)}) collective-permute-start(s32[48,2]{0,1:T(2,128)} %bitcast.26), channel_id=1, source_target_pairs={{0,4},{4,0},{8,12},{12,8},{16,20},{20,16},{24,28},{28,24},{1,5},{5... | collective-permute-start | bytes 1160 | tf_op jit(solution)/shard_map/ppermute | solution.py:19
  703.1 228.4 %collective-permute-start.3 = (f32[2048]{0:T(1024)S(1)}, f32[2048]{0:T(1024)S(1)}, u32[]{:S(2)}, u32[]{:S(2)}) collective-permute-start(f32[2048]{0:T(1024)S(1)} %get-tuple-element.1066), channel_id=1, source_target_pairs={{0,4},{4,0},{8,12},{12,8},{16,20},{20,16},{24,28},{28,24},{1,5},{5... | collective-permute-start | bytes 24584 | tf_op jit(solution)/shard_map/ppermute | solution.py:19
  703.3 228.1 %collective-permute-start.4 = (f32[3,2048]{1,0:T(4,128)S(1)}, f32[3,2048]{1,0:T(4,128)S(1)}, u32[]{:S(2)}, u32[]{:S(2)}) collective-permute-start(f32[3,2048]{1,0:T(4,128)S(1)} %get-tuple-element.1063), channel_id=1, source_target_pairs={{0,4},{4,0},{8,12},{12,8},{16,20},{20,16},{24,28},{28,24},{1,5},{5... | collective-permute-start | bytes 73736 | tf_op jit(solution)/shard_map/ppermute | solution.py:19
  918.1 4.0 copy-start
  930.7 104.3 %collective-permute-start.2 = (bf16[2048,512]{1,0:T(8,128)(2,1)}, bf16[2048,512]{1,0:T(8,128)(2,1)}, u32[]{:S(2)}, u32[]{:S(2)}) collective-permute-start(bf16[2048,512]{1,0:T(8,128)(2,1)} %get-tuple-element.921), channel_id=1, source_target_pairs={{0,4},{4,0},{8,12},{12,8},{16,20},{20,16},{24,28},{28,24},{1,5},{5... | collective-permute-start | bytes 6291464 | tf_op jit(solution)/shard_map/ppermute | solution.py:19
  931.5 3.0 copy-start.4
  931.5 3.0 copy-start.6
Sparse Core Ops, SparseCore 0:
  310.0 379.7 all-reduce.3
  701.4 77.2 all-reduce.5
  1035.2 222.9 reduce-scatter.1
where the time goes:
time: 1280 us; the launch traced here: 1270 us
  waiting for transfers between devices  671 us (52%)
  other arithmetic  175 us (14%)
  local copies, waits for them, and re-layouts  145 us (11%)
  matrix products  128 us (10%)
  loops' own time  123 us (10%)
  between operations  19.2 us (2%)
    psum x1, waiting for transfers between devices, per_device(): whole_y = lax.psum(partial_y, 'cols')  380 us
    reduce_scatter x1, waiting for transfers between devices, per_device(): lax.psum_scatter(add_products(running, partner_basis, partner_cache, part...  221 us
    another operation x14, other arithmetic, basis_map(): lower = jnp.linalg.cholesky(gram_total)  80.4 us
    psum x1, waiting for transfers between devices, per_device(): gram_total = lax.psum(gram_local(whole_y), 'rows')  70.4 us
    dot_general x24, matrix products, sketch_step(): jnp.dot(cache_tiles[slot_index], sketch_part, preferred_element_type=jnp....  53.4 us
    dot_general x21, matrix products, product_step(): lax.dot_general(basis_part, cache_tiles[slot_index], (((0,), (0,)), ((),...  48.4 us
    another operation x1, loops' own time, sketch_partial(): lax.fori_loop(0, slot_stop, sketch_step, jnp.zeros((local_rows, gauss_ske...  48.2 us
    dynamic_update_slice x24, other arithmetic, cache_step(): lax.dynamic_update_slice_in_dim(cached, fresh_tile[None], slot_index, 0)  47.7 us
  transfers between devices with their start and end apart: 8, of which 3 were waited for; matrix products, arithmetic and copies ran while one was open for 18% of the time, Pallas kernels for 0%

commit v1 on v0

v1 whole, which is shorter than its diff:
```python
import functools
import math

import jax
import jax.numpy as jnp
import numpy as np
from jax import lax
from jax.experimental import pallas as pl
from jax.experimental.pallas import tpu as pltpu
from jax.sharding import PartitionSpec as P

TILE = 256


WAVENUMBER = 150.0
WALL_GAP = 2.0
HIGHEST = lax.Precision.HIGHEST
CHUNK = 32
TURN_HIGH = 6.28125
TURN_LOW = float(2.0 * np.pi - 6.28125)


def half_cos_terms(degree=4):
    top = np.pi**2 * 1.0001
    series = np.polynomial.Chebyshev.interpolate(
        lambda w: np.cos(np.sqrt(np.maximum(w, 0.0)) / 2.0), degree, domain=[0.0, top]
    )
    return [float(c) for c in series.convert(kind=np.polynomial.Polynomial).coef]


def tile_values(row_part, col_part):
    diff_x = row_part[:, 0:1] - col_part[0:1, :]
    diff_y = row_part[:, 1:2] - col_part[1:2, :]
    diff_z = row_part[:, 2:3] - col_part[2:3, :] - WALL_GAP
    square = diff_x * diff_x + diff_y * diff_y + diff_z * diff_z
    inverse = lax.rsqrt(square)
    distance = square * inverse
    distance = distance + (0.5 * inverse) * (square - distance * distance)
    angle = WAVENUMBER * distance
    turns = jnp.floor(angle * float(0.5 / np.pi) + 0.5)
    rest = (angle - turns * TURN_HIGH) - turns * TURN_LOW
    w = rest * rest
    terms = half_cos_terms()
    half = jnp.full_like(w, terms[-1])
    for term in terms[-2::-1]:
        half = half * w + term
    cosine = 2.0 * (half * half) - 1.0
    return (row_part[:, 3:4] * col_part[3:4, :]) * cosine * inverse


def tiles_kernel(list_ref, count_ref, rows_ref, walls_ref, matrix_ref):
    tile = walls_ref.shape[2]
    matrix_ref[...] = jnp.zeros_like(matrix_ref)

    def slot(index, carry):
        row_block = list_ref[index, 0]
        col_block = list_ref[index, 1]
        col_part = walls_ref[col_block]

        def chunk(step, inner):
            start = pl.multiple_of(row_block * tile + step * CHUNK, CHUNK)
            values = tile_values(rows_ref[pl.ds(start, CHUNK), :], col_part)
            matrix_ref[col_block, pl.ds(start, CHUNK), :] = values.astype(jnp.bfloat16)
            return inner

        return lax.fori_loop(0, tile // CHUNK, chunk, carry, unroll=2)

    lax.fori_loop(0, count_ref[0], slot, 0)


def dense_tiles(capsule_points, capsule_weight, wall_points, wall_weight, local_list, count):
    local_rows = capsule_points.shape[1]
    col_blocks = wall_points.shape[1] // TILE
    rows = jnp.concatenate([capsule_points, capsule_weight[None]], axis=0).T
    walls = jnp.concatenate([wall_points, wall_weight[None]], axis=0)
    walls = walls.reshape(4, col_blocks, TILE).transpose(1, 0, 2)
    smem = pl.BlockSpec(memory_space=pltpu.SMEM)
    vmem = pl.BlockSpec(memory_space=pltpu.VMEM)
    return pl.pallas_call(
        tiles_kernel,
        out_shape=jax.ShapeDtypeStruct((col_blocks, local_rows, TILE), jnp.bfloat16),
        in_specs=[smem, smem, vmem, vmem],
        out_specs=vmem,
        compiler_params=pltpu.CompilerParams(vmem_limit_bytes=40 * 2**20),
    )(local_list, count, rows, walls)


def basis_map(gram_total, identity):
    lower = jnp.linalg.cholesky(gram_total)
    inverse = jax.scipy.linalg.solve_triangular(lower, identity, lower=True)
    return inverse.T


def per_device(
    capsule_points, capsule_weight, wall_points, wall_weight, gauss_sketch, far_pairs, tile_count
):
    row_dev = lax.axis_index("rows")
    col_dev = lax.axis_index("cols")
    local_rows = capsule_points.shape[1]
    wall_cells = wall_points.shape[1]
    row_blocks = local_rows // TILE
    col_blocks = wall_cells // TILE
    samples = gauss_sketch.shape[1]
    offset = jnp.stack([row_dev * row_blocks, col_dev * col_blocks]).astype(jnp.int32)
    matrix = dense_tiles(
        capsule_points,
        capsule_weight,
        wall_points,
        wall_weight,
        far_pairs[0, 0] - offset[None, :],
        tile_count[0],
    )
    partial_y = lax.dot_general(
        matrix,
        gauss_sketch.reshape(col_blocks, TILE, samples),
        (((0, 2), (0, 1)), ((), ())),
        preferred_element_type=jnp.float32,
    )
    basis_scale = math.sqrt(local_rows * lax.axis_size("rows"))
    share_y = lax.psum_scatter(partial_y, "cols", scatter_dimension=0, tiled=True)
    gram = lax.dot_general(
        share_y,
        share_y,
        (((0,), (0,)), ((), ())),
        precision=HIGHEST,
        preferred_element_type=jnp.float32,
    )
    gram_total = lax.psum(gram, ("rows", "cols"))
    share_q = jnp.dot(
        share_y,
        basis_map(gram_total, jnp.eye(samples, dtype=jnp.float32)),
        precision=HIGHEST,
        preferred_element_type=jnp.float32,
    )
    basis_out = (basis_scale * share_q).astype(jnp.bfloat16)
    q_round = lax.all_gather(share_q.astype(jnp.bfloat16), "cols", axis=0, tiled=True)
    partial_p = lax.dot_general(
        q_round, matrix, (((0,), (1,)), ((), ())), preferred_element_type=jnp.float32
    ).reshape(samples, wall_cells)
    projected = lax.psum_scatter(partial_p, "rows", scatter_dimension=0, tiled=True)
    return (basis_out, projected)


def solution(mesh):
    placed = (
        P(None, "rows"),
        P("rows"),
        P(None, "cols"),
        P("cols"),
        P("cols", None),
        P("rows", "cols", None, None),
        P("rows", "cols"),
    )
    return jax.shard_map(
        per_device,
        mesh=mesh,
        in_specs=placed,
        out_specs=(P(("rows", "cols"), None), P("rows", "cols")),
        check_vma=False,
    )
```

time: 1280 us -> 530 us (0.41)
  waiting for transfers between devices: 671 us -> 285 us
  loops' own time: 123 us -> 0.01 us
  local copies, waits for them, and re-layouts: 145 us -> 26.9 us
  matrix products: 128 us -> 36.1 us
  other arithmetic: 175 us -> 127 us
  Pallas kernels: 0 us -> 29.8 us
    psum x2 -> x1, waiting for transfers between devices: 450 us -> 127 us  [per_device(): gram_total = lax.psum(gram, ('rows', 'cols'))]
    another operation x5 -> x0, loops' own time: 123 us -> none  [the longest x1 48.2 us: sketch_partial(): lax.fori_loop(0, slot_stop, sketch_step, jnp.zeros((local_rows, gauss_ske...]
    dynamic_slice x186 -> x0, local copies, waits for them, and re-layouts: 102 us -> none  [the longest x48 20 us: cut_block(): lax.dynamic_slice_in_dim(weights, first_cell, tile_width, 0)]
    dot_general x47 -> x4, matrix products: 122 us -> 23.8 us  [the longest x1 10.5 us: per_device(): lax.dot_general(q_round, matrix, (((0,), (1,)), ((), ())), preferred_elem...]
    reduce_scatter x1 -> x2, waiting for transfers between devices: 221 us -> 133 us  [the longest x1 87.7 us: per_device(): lax.psum_scatter(partial_p, 'rows', scatter_dimension=0, tiled=True)]
    dynamic_update_slice x24 -> x0, other arithmetic: 47.7 us -> none  [cache_step(): lax.dynamic_update_slice_in_dim(cached, fresh_tile[None], slot_index, 0)]
    pallas_call x0 -> x1, Pallas kernels: none -> 29.8 us  [dense_tiles(): pl.pallas_call(tiles_kernel, out_shape=jax.ShapeDtypeStruct((col_blocks,...]
    all_gather x0 -> x1, waiting for transfers between devices: none -> 24.1 us  [per_device(): lax.all_gather(share_q.astype(jnp.bfloat16), 'cols', axis=0, tiled=True)]
  transfers between devices with their start and end apart: 8 -> 4, of which waited for: 3 -> 4; matrix products, arithmetic and copies ran while one was open for 18% -> 0% of each run, Pallas kernels for 0% -> 0%
where the time goes in v1:
time: 530 us; the launch traced here: 522 us
  waiting for transfers between devices  285 us (54%)
  other arithmetic  127 us (24%)
  matrix products  36.1 us (7%)
  Pallas kernels  29.8 us (6%)
  local copies, waits for them, and re-layouts  26.9 us (5%)
  between operations  17.4 us (3%)
    psum x1, waiting for transfers between devices, per_device(): gram_total = lax.psum(gram, ('rows', 'cols'))  127 us
    reduce_scatter x1, waiting for transfers between devices, per_device(): lax.psum_scatter(partial_p, 'rows', scatter_dimension=0, tiled=True)  87.7 us
    another operation x14, other arithmetic, basis_map(): lower = jnp.linalg.cholesky(gram_total)  79.2 us
    reduce_scatter x1, waiting for transfers between devices, per_device(): lax.psum_scatter(partial_y, 'cols', scatter_dimension=0, tiled=True)  45.7 us
    another operation x3, other arithmetic, basis_map(): inverse = jax.scipy.linalg.solve_triangular(lower, identity, lower=True)  42.5 us
    pallas_call x1, Pallas kernels, dense_tiles(): pl.pallas_call(tiles_kernel, out_shape=jax.ShapeDtypeStruct((col_blocks,...  29.8 us
    all_gather x1, waiting for transfers between devices, per_device(): lax.all_gather(share_q.astype(jnp.bfloat16), 'cols', axis=0, tiled=True)  24.1 us
    another operation x12, local copies, waits for them, and re-layouts  14.3 us
  transfers between devices with their start and end apart: 4, of which 4 were waited for; matrix products, arithmetic and copies ran while one was open for 0% of the time, Pallas kernels for 0%

profile of v1, /device:TPU:11, one launch (start us, length us, event | category | flops | bytes accessed | tf_op | source)
XLA Modules:
  0.0 522.1 jit_solution(16338856723587722246)
XLA Ops:
  7.2 0.9 copy.28
  8.8 0.8 pad_maximum_fusion
  10.0 0.8 maximum_bitcast_fusion.walls_ref
  10.8 29.8 %shard_map.86 = bf16[8,2048,256]{2,1,0:T(8,128)(2,1)S(1)} custom-call(s32[48,2]{1,0:T(8,128)S(1)} %broadcast_subtract_fusion.list_ref, s32[1]{0:T(128)} %bitcast.71.count_ref, f32[2048,4]{1,0:T(8,128)S(1)} %bitcast.73, f32[8,4,256]{2,1,0:T(4,128)S(1)} %maximum_bitcast_fusion.walls_ref), custom_call_target="tpu_custom_call" | custom-call | tf_op jit(solution)/shard_map/pallas_call | solution.py:79
  40.7 3.2 copy-done.1
  43.9 5.9 %convolution_bitcast_fusion = f32[2048,512]{1,0:T(8,128)} fusion(bf16[8,2048,256]{2,1,0:T(8,128)(2,1)S(1)} %shard_map.86, bf16[8,256,512]{2,1,0:T(8,128)(2,1)S(1)} %bitcast.72), kind=kOutput, calls=%fused_computation.2 | convolution fusion | flops 4294967296 | bytes 14680064 | tf_op jit(solution)/shard_map/dot_general | solution.py:113
  49.9 45.7 %reduce-scatter.3.cloned.1.call-done = f32[512,512]{1,0:T(8,128)} async-done(((f32[2048,512]{1,0:T(8,128)}), f32[512,512]{1,0:T(8,128)}) %reduce-scatter.3.cloned.1.call-update) | async-done | bytes 1048592 | tf_op jit(solution)/shard_map/reduce_scatter | solution.py:120
  95.6 4.5 fusion.44
  100.4 0.8 iota_compare_fusion
  101.2 1.2 fusion.19
  102.4 127.1 %all-reduce.3.cloned.1.call-done = f32[512,512]{0,1:T(8,128)} async-done(((f32[512,512]{0,1:T(8,128)}), f32[512,512]{0,1:T(8,128)}) %all-reduce.3.cloned.1.call-update) | async-done | bytes 1048592 | tf_op jit(solution)/shard_map/psum | solution.py:128
  229.5 1.6 copy.32
  231.1 1.4 fusion.10
  232.5 1.0 copy-done.4
  233.5 11.7 %cholesky.104 = f32[128,128]{1,0:T(8,128)S(1)} custom-call(f32[128,128]{1,0:T(8,128)S(1)} %cholesky.266), custom_call_target="Cholesky" | custom-call | tf_op jit(solution)/shard_map/jit(cholesky)/cholesky | solution.py:89
  245.4 9.8 %custom-call.31 = f32[1,128,128]{1,2,0:T(8,128)S(1)} custom-call(f32[1,128,128]{2,1,0:T(8,128)S(1)} %get-tuple-element.31), custom_call_target="InvertDiagBlocksLowerTriangular" | custom-call | tf_op jit(solution)/shard_map/jit(cholesky)/cholesky | solution.py:89
  255.2 1.2 constant_dynamic-update-slice_fusion.3
  256.5 1.3 convolution_subtract_fusion.3
  257.7 11.7 %cholesky.217 = f32[128,128]{1,0:T(8,128)S(1)} custom-call(f32[128,128]{1,0:T(8,128)S(1)} %cholesky.270), custom_call_target="Cholesky" | custom-call | tf_op jit(solution)/shard_map/jit(cholesky)/cholesky | solution.py:89
  269.5 10.2 %custom-call.32 = f32[1,128,128]{1,2,0:T(8,128)S(1)} custom-call(f32[1,128,128]{2,1,0:T(8,128)S(1)} %get-tuple-element.28), custom_call_target="InvertDiagBlocksLowerTriangular" | custom-call | tf_op jit(solution)/shard_map/jit(cholesky)/cholesky | solution.py:89
  279.9 1.3 convolution_subtract_fusion.4
  281.2 11.7 %cholesky.238 = f32[128,128]{1,0:T(8,128)S(1)} custom-call(f32[128,128]{1,0:T(8,128)S(1)} %cholesky.275), custom_call_target="Cholesky" | custom-call | tf_op jit(solution)/shard_map/jit(cholesky)/cholesky | solution.py:89
  293.0 9.8 %custom-call.33 = f32[1,128,128]{1,2,0:T(8,128)S(1)} custom-call(f32[1,128,128]{2,1,0:T(8,128)S(1)} %get-tuple-element.25), custom_call_target="InvertDiagBlocksLowerTriangular" | custom-call | tf_op jit(solution)/shard_map/jit(cholesky)/cholesky | solution.py:89
  303.0 1.2 convolution_subtract_fusion.5
  304.3 11.7 %cholesky.255 = f32[128,128]{1,0:T(8,128)S(1)} custom-call(f32[128,128]{1,0:T(8,128)S(1)} %convolution_subtract_fusion.5), custom_call_target="Cholesky" | custom-call | tf_op jit(solution)/shard_map/jit(cholesky)/cholesky | solution.py:89
  316.0 0.9 compare_reduce_fusion.1
  316.9 0.8 compare_reduce_fusion
  317.7 0.7 compare_reduce_fusion.2
  321.0 2.4 select_select_fusion
  323.4 14.3 %while.1 = (s32[]{:T(128)}, f32[512,512]{1,0:T(8,128)}, s32[4,2]{0,1:T(2,128)S(1)}, f32[4,128,128]{2,1,0:T(8,128)}, s32[]{:T(128)}) while((s32[]{:T(128)}, f32[512,512]{1,0:T(8,128)}, s32[4,2]{0,1:T(2,128)S(1)}, f32[4,128,128]{2,1,0:T(8,128)}, s32[]{:T(128)}) %tuple.32), condition=%wide.while_cond, body=%wide.while_body.sunk | while | flops 2 | bytes 132205 | solution.py:90
  323.5 0.6 fusion.57
  324.0 2.9 bitcast_dynamic-update-slice_fusion.2
  327.1 0.6 fusion.57
  327.6 2.9 bitcast_dynamic-update-slice_fusion.2
  330.7 0.6 fusion.57
  331.2 2.9 bitcast_dynamic-update-slice_fusion.2
  334.3 0.6 fusion.57
  334.8 2.9 bitcast_dynamic-update-slice_fusion.2
  337.7 40.1 %custom-call.34 = f32[4,128,128]{1,2,0:T(8,128)S(1)} custom-call(f32[4,128,128]{2,1,0:T(8,128)} %get-tuple-element.9), custom_call_target="InvertDiagBlocksLowerTriangular" | custom-call | tf_op jit(solution)/shard_map/jit(_solve_triangular)/triangular_solve | solution.py:90
  377.8 1.1 fusion.21
  378.9 1.4 convolution_subtract_fusion.1
  380.7 1.4 convolution_subtract_fusion
  382.6 1.7 convolution_subtract_fusion.2
  384.7 2.8 fusion.43
  387.6 24.1 %all-gather.2.cloned.1.call-done = bf16[2048,512]{1,0:T(8,128)(2,1)} async-done(((bf16[512,512]{1,0:T(8,128)(2,1)}), bf16[2048,512]{1,0:T(8,128)(2,1)}) %all-gather.2.cloned.1.call-update) | async-done | bytes 2097168 | tf_op jit(solution)/shard_map/all_gather | solution.py:136
  411.7 10.5 %fusion = f32[512,8,256]{0,2,1:T(8,128)} fusion(bf16[8,2048,256]{2,1,0:T(8,128)(2,1)} %copy-done.1, bf16[2048,512]{1,0:T(8,128)(2,1)} %all-gather.2.cloned.1.call-done), kind=kOutput, calls=%fused_computation.3 | convolution fusion | flops 4294967296 | bytes 14680064 | tf_op jit(solution)/shard_map/dot_general | solution.py:137
  422.2 5.4 %copy.34 = f32[512,2048]{1,0:T(8,128)} copy(f32[512,2048]{0,1:T(8,128)} %bitcast.74) | data formatting | bytes 8388608 | tf_op jit(solution)/shard_map/reshape | solution.py:139
  427.6 87.7 %reduce-scatter.5.cloned.1.call-done = f32[64,2048]{1,0:T(8,128)} async-done(((f32[512,2048]{1,0:T(8,128)}), f32[64,2048]{1,0:T(8,128)}) %reduce-scatter.5.cloned.1.call-update) | async-done | bytes 524304 | tf_op jit(solution)/shard_map/reduce_scatter | solution.py:140
  (39 shorter events, 3.2 us)
Async XLA Ops:
  7.2 33.5 %copy-start = (bf16[2048,512]{1,0:T(8,128)(2,1)S(1)}, bf16[2048,512]{1,0:T(8,128)(2,1)}, u32[]{:S(2)}) copy-start(bf16[2048,512]{1,0:T(8,128)(2,1)} %param.11) | copy-start | bytes 6291460
  7.2 88.5 %reduce-scatter.3.cloned.1.call-start = ((), (), s32[]{:S(2)}) async-start(), calls=%async_computation.2 | async-start | bytes 5242880 | tf_op jit(solution)/shard_map/reduce_scatter | solution.py:120
  40.7 3.2 copy-start.1
  49.9 179.6 %all-reduce.3.cloned.1.call-start = ((), (), s32[]{:S(2)}) async-start(), calls=%async_computation.3 | async-start | bytes 2097152 | tf_op jit(solution)/shard_map/psum | solution.py:128
  100.2 311.5 %all-gather.2.cloned.1.call-start = ((), (), s32[]{:S(2)}) async-start(), calls=%async_computation.4 | async-start | bytes 2621440 | tf_op jit(solution)/shard_map/all_gather | solution.py:136
  232.5 1.0 copy-start.4
  316.0 4.9 copy-start.3
  320.9 63.8 %copy-start.2 = (f32[512,512]{1,0:T(8,128)S(1)}, f32[512,512]{1,0:T(8,128)}, u32[]{:S(2)}) copy-start(f32[512,512]{1,0:T(8,128)} %reduce-scatter.3.cloned.1.call-done) | copy-start | bytes 3145732
  387.6 127.7 %reduce-scatter.5.cloned.1.call-start = ((), (), s32[]{:S(2)}) async-start(), calls=%async_computation.5 | async-start | bytes 4718592 | tf_op jit(solution)/shard_map/reduce_scatter | solution.py:140
Sparse Core Ops, SparseCore 0:
  50.0 45.5 reduce-scatter.2
  101.6 127.8 all-reduce.2
  387.7 23.9 all-gather.1
  427.7 87.5 reduce-scatter.4

commit v2 on v1

--- a/solution.py
+++ b/solution.py
@@ -85,10 +85,314 @@
     )(local_list, count, rows, walls)
 
 
-def basis_map(gram_total, identity):
-    lower = jnp.linalg.cholesky(gram_total)
-    inverse = jax.scipy.linalg.solve_triangular(lower, identity, lower=True)
-    return inverse.T
+PANEL = 8
+BLOCK = 128
+
+
+def full_dot(left, right, left_dim, right_dim):
+    return lax.dot_general(
+        left,
+        right,
+        (((left_dim,), (right_dim,)), ((), ())),
+        precision=HIGHEST,
+        preferred_element_type=jnp.float32,
+    )
+
+
+def eliminate_panel(panel, first):
+    lanes = lax.broadcasted_iota(jnp.int32, (PANEL, BLOCK), 1)
+    subs = lax.broadcasted_iota(jnp.int32, (PANEL, BLOCK), 0)
+    left = panel[:, :BLOCK]
+    right = panel[:, BLOCK:]
+    columns = [
+        jnp.broadcast_to(
+            jnp.sum(jnp.where(lanes == first + j, left, 0.0), axis=1, keepdims=True),
+            (PANEL, BLOCK),
+        )
+        for j in range(PANEL)
+    ]
+    for j in range(PANEL):
+        pivot = jnp.broadcast_to(columns[j][j : j + 1, :], (PANEL, BLOCK))
+        scale = lax.rsqrt(pivot)
+        scale = scale * (1.5 - 0.5 * pivot * (scale * scale))
+        multiplier = columns[j] * scale
+
+        def step(value):
+            row = jnp.broadcast_to(value[j : j + 1, :], (PANEL, BLOCK)) * scale
+            return jnp.where(subs == j, row, jnp.where(subs > j, value - multiplier * row, value))
+
+        left = step(left)
+        right = step(right)
+        for k in range(j + 1, PANEL):
+            columns[k] = step(columns[k])
+    return left, right
+
+
+def inverse_kernel(gram_ref, inverse_ref, work, small):
+    size = gram_ref.shape[0]
+    lanes = lax.broadcasted_iota(jnp.int32, (PANEL, BLOCK), 1)
+    rows_eye = lax.broadcasted_iota(jnp.int32, (BLOCK, BLOCK), 0)
+    cols_eye = lax.broadcasted_iota(jnp.int32, (BLOCK, BLOCK), 1)
+    eye = jnp.where(rows_eye == cols_eye, 1.0, 0.0).astype(jnp.float32)
+    work[:, :size] = gram_ref[...]
+    work[:, size:] = jnp.zeros((size, size), jnp.float32)
+    inverse_ref[...] = jnp.zeros_like(inverse_ref)
+    for start in range(0, size, BLOCK):
+        stop = start + BLOCK
+        small[:, :BLOCK] = work[start:stop, start:stop]
+        small[:, BLOCK:] = eye
+
+        def group(index, carry):
+            first = pl.multiple_of(index * PANEL, PANEL)
+            left, right = eliminate_panel(small[pl.ds(first, PANEL), :], first)
+            both = jnp.concatenate([left, right], axis=1)
+            below = jnp.where(lanes >= first + PANEL, left, 0.0)
+            small[...] = small[...] - full_dot(below, both, 0, 0)
+            small[pl.ds(first, PANEL), :] = both
+            return carry
+
+        lax.fori_loop(0, BLOCK // PANEL, group, 0)
+        block_inverse = small[:, BLOCK:]
+        if start:
+            known = full_dot(block_inverse, work[start:stop, size : size + start], 1, 0)
+            inverse_ref[start:stop, :start] = known
+        inverse_ref[start:stop, start:stop] = block_inverse
+        if stop < size:
+            ahead = full_dot(block_inverse, work[start:stop, stop:size], 1, 0)
+            done = inverse_ref[start:stop, :stop]
+            work[stop:, stop:size] = work[stop:, stop:size] - full_dot(ahead, ahead, 0, 0)
+            work[stop:, size : size + stop] = work[stop:, size : size + stop] - full_dot(
+                ahead, done, 0, 0
+            )
+
+
+def lower_inverse(gram_total):
+    size = gram_total.shape[0]
+    vmem = pl.BlockSpec(memory_space=pltpu.VMEM)
+    return pl.pallas_call(
+        inverse_kernel,
+        out_shape=jax.ShapeDtypeStruct((size, size), jnp.float32),
+        in_specs=[vmem],
+        out_specs=vmem,
+        scratch_shapes=[
+            pltpu.VMEM((size, 2 * size), jnp.float32),
+            pltpu.VMEM((BLOCK, 2 * BLOCK), jnp.float32),
+        ],
+        compiler_params=pltpu.CompilerParams(vmem_limit_bytes=32 * 2**20),
+    )(gram_total)
+
+
+def greet(peers):
+    barrier = pltpu.get_barrier_semaphore()
+    for peer in peers:
+        pl.semaphore_signal(
+            barrier, inc=1, device_id=peer, device_id_type=pl.DeviceIdType.MESH
+        )
+    pl.semaphore_wait(barrier, len(peers))
+
+
+def send(source, target, send_sem, recv_sem, peer):
+    copy = pltpu.make_async_remote_copy(
+        src_ref=source,
+        dst_ref=target,
+        send_sem=send_sem,
+        recv_sem=recv_sem,
+        device_id=peer,
+        device_id_type=pl.DeviceIdType.MESH,
+    )
+    copy.start()
+    return copy
+
+
+def wait_all(copies):
+    for copy in copies:
+        copy.wait()
+
+
+def sketch_kernel(
+    n_rows,
+    n_cols,
+    y_ref,
+    share_ref,
+    gram_ref,
+    totals,
+    first_in,
+    later_out,
+    later_in,
+    gram_own,
+    col_in,
+    row_sum,
+    row_in,
+    whole,
+    first_send,
+    first_recv,
+    later_send,
+    later_recv,
+    col_send,
+    col_recv,
+    row_send,
+    row_recv,
+):
+    me_row = lax.axis_index("rows")
+    me_col = lax.axis_index("cols")
+    row_peers = [
+        (lax.rem(me_row + d, n_rows), me_col) for d in range(1, n_rows)
+    ]
+    col_peers = [
+        (me_row, lax.rem(me_col + d, n_cols)) for d in range(1, n_cols)
+    ]
+    greet(row_peers + col_peers)
+
+    half = n_cols // 2
+    bit = me_col % 2
+    other = (me_row, me_col + 1 - 2 * bit)
+    copies = [
+        send(y_ref.at[1 - bit + 2 * j], first_in.at[j], first_send.at[j], first_recv.at[j], other)
+        for j in range(half)
+    ]
+    for j in range(half):
+        copies[j].wait()
+        totals[j] = y_ref[bit + 2 * j] + first_in[j]
+    stride, slot = 1, 0
+    while stride < half:
+        low = (me_col // 2) % stride
+        bit = (me_col // (2 * stride)) % 2
+        other = (me_row, me_col + 2 * stride * (1 - 2 * bit))
+        copies = []
+        base = slot
+        for j in range(half // (2 * stride)):
+            source = low + stride * (1 - bit) + 2 * stride * j
+            later_out[slot] = totals[source].astype(jnp.bfloat16)
+            copies.append(
+                send(
+                    later_out.at[slot],
+                    later_in.at[slot],
+                    later_send.at[slot],
+                    later_recv.at[slot],
+                    other,
+                )
+            )
+            slot += 1
+        for j, copy in enumerate(copies):
+            copy.wait()
+            kept = low + stride * bit + 2 * stride * j
+            totals[kept] = totals[kept] + later_in[base + j].astype(jnp.float32)
+        stride *= 2
+    share = totals[me_col // 2]
+    share_ref[...] = share
+
+    gram = full_dot(share, share, 0, 0)
+    gram_own[...] = gram.reshape(gram_own.shape)
+    copies = [
+        send(gram_own.at[peer[1]], col_in.at[d], col_send.at[0, d], col_recv.at[0, d], peer)
+        for d, peer in enumerate(col_peers)
+    ]
+    wait_all(copies)
+    total = gram_own[me_col]
+    for d in range(n_cols - 1):
+        total = total + col_in[d]
+    row_sum[...] = total
+    copies = [
+        send(row_sum.at[peer[0]], row_in.at[d], row_send.at[0, d], row_recv.at[0, d], peer)
+        for d, peer in enumerate(row_peers)
+    ]
+    wait_all(copies)
+    total = row_sum[me_row]
+    for d in range(n_rows - 1):
+        total = total + row_in[d]
+    whole[me_col, me_row] = total
+    mine = whole.at[me_col, me_row]
+    copies = [
+        send(mine, mine, row_send.at[1, d], row_recv.at[1, d], peer)
+        for d, peer in enumerate(row_peers)
+    ]
+    wait_all(copies)
+    mine = whole.at[me_col]
+    copies = [
+        send(mine, mine, col_send.at[1, d], col_recv.at[1, d], peer)
+        for d, peer in enumerate(col_peers)
+    ]
+    wait_all(copies)
+    gram_ref[...] = whole[...]
+
+
+def sketch_and_gram(partial_y):
+    n_rows, n_cols = lax.axis_size("rows"), lax.axis_size("cols")
+    local_rows, samples = partial_y.shape
+    share = local_rows // n_cols
+    half = n_cols // 2
+    part = samples // (n_rows * n_cols)
+    vmem = pl.BlockSpec(memory_space=pltpu.VMEM)
+    later = max(half - 1, 1)
+    dma = pltpu.SemaphoreType.DMA
+    share_y, gram = pl.pallas_call(
+        functools.partial(sketch_kernel, n_rows, n_cols),
+        out_shape=(
+            jax.ShapeDtypeStruct((share, samples), jnp.float32),
+            jax.ShapeDtypeStruct((n_cols, n_rows, part, samples), jnp.float32),
+        ),
+        in_specs=[vmem],
+        out_specs=(vmem, vmem),
+        scratch_shapes=[
+            pltpu.VMEM((half, share, samples), jnp.float32),
+            pltpu.VMEM((half, share, samples), jnp.float32),
+            pltpu.VMEM((later, share, samples), jnp.bfloat16),
+            pltpu.VMEM((later, share, samples), jnp.bfloat16),
+            pltpu.VMEM((n_cols, n_rows, part, samples), jnp.float32),
+            pltpu.VMEM((n_cols - 1, n_rows, part, samples), jnp.float32),
+            pltpu.VMEM((n_rows, part, samples), jnp.float32),
+            pltpu.VMEM((n_rows - 1, part, samples), jnp.float32),
+            pltpu.VMEM((n_cols, n_rows, part, samples), jnp.float32),
+            dma((half,)),
+            dma((half,)),
+            dma((later,)),
+            dma((later,)),
+            dma((2, n_cols - 1)),
+            dma((2, n_cols - 1)),
+            dma((2, n_rows - 1)),
+            dma((2, n_rows - 1)),
+        ],
+        compiler_params=pltpu.CompilerParams(
+            collective_id=0, has_side_effects=True, vmem_limit_bytes=48 * 2**20
+        ),
+    )(partial_y.reshape(n_cols, share, samples))
+    return share_y, gram.reshape(samples, samples)
+
+
+def project_kernel(n_rows, p_ref, out_ref, arrived, send_sem, recv_sem):
+    me_row = lax.axis_index("rows")
+    me_col = lax.axis_index("cols")
+    peers = [(lax.rem(me_row + d, n_rows), me_col) for d in range(1, n_rows)]
+    greet(peers)
+    copies = [
+        send(p_ref.at[peer[0]], arrived.at[d], send_sem.at[d], recv_sem.at[d], peer)
+        for d, peer in enumerate(peers)
+    ]
+    out_ref[...] = p_ref[me_row].astype(jnp.float32)
+    for d, copy in enumerate(copies):
+        copy.wait()
+        out_ref[...] += arrived[d].astype(jnp.float32)
+
+
+def project_scatter(partial_p):
+    n_rows = lax.axis_size("rows")
+    samples, wall_cells = partial_p.shape
+    part = samples // n_rows
+    vmem = pl.BlockSpec(memory_space=pltpu.VMEM)
+    return pl.pallas_call(
+        functools.partial(project_kernel, n_rows),
+        out_shape=jax.ShapeDtypeStruct((part, wall_cells), jnp.float32),
+        in_specs=[vmem],
+        out_specs=vmem,
+        scratch_shapes=[
+            pltpu.VMEM((n_rows - 1, part, wall_cells), jnp.bfloat16),
+            pltpu.SemaphoreType.DMA((n_rows - 1,)),
+            pltpu.SemaphoreType.DMA((n_rows - 1,)),
+        ],
+        compiler_params=pltpu.CompilerParams(
+            collective_id=1, has_side_effects=True, vmem_limit_bytes=32 * 2**20
+        ),
+    )(partial_p.reshape(n_rows, part, wall_cells))
 
 
 def per_device(
@@ -117,27 +421,14 @@
         preferred_element_type=jnp.float32,
     )
     basis_scale = math.sqrt(local_rows * lax.axis_size("rows"))
-    share_y = lax.psum_scatter(partial_y, "cols", scatter_dimension=0, tiled=True)
-    gram = lax.dot_general(
-        share_y,
-        share_y,
-        (((0,), (0,)), ((), ())),
-        precision=HIGHEST,
-        preferred_element_type=jnp.float32,
-    )
-    gram_total = lax.psum(gram, ("rows", "cols"))
-    share_q = jnp.dot(
-        share_y,
-        basis_map(gram_total, jnp.eye(samples, dtype=jnp.float32)),
-        precision=HIGHEST,
-        preferred_element_type=jnp.float32,
-    )
+    share_y, gram_total = sketch_and_gram(partial_y)
+    share_q = full_dot(share_y, lower_inverse(gram_total), 1, 1)
     basis_out = (basis_scale * share_q).astype(jnp.bfloat16)
     q_round = lax.all_gather(share_q.astype(jnp.bfloat16), "cols", axis=0, tiled=True)
     partial_p = lax.dot_general(
         q_round, matrix, (((0,), (1,)), ((), ())), preferred_element_type=jnp.float32
     ).reshape(samples, wall_cells)
-    projected = lax.psum_scatter(partial_p, "rows", scatter_dimension=0, tiled=True)
+    projected = project_scatter(partial_p.astype(jnp.bfloat16))
     return (basis_out, projected)
 
 

time: 530 us -> 251 us (0.47); the launches traced: 522 us -> 253 us
  waiting for transfers between devices: 285 us -> 23.3 us
  Pallas kernels: 29.8 us -> 182 us
  other arithmetic: 127 us -> 1.67 us
  matrix products: 36.1 us -> 17.3 us
  local copies, waits for them, and re-layouts: 26.9 us -> 13.5 us
    pallas_call x0 -> x3, Pallas kernels: none -> 165 us  [the longest x1 79.4 us: sketch_and_gram(): pl.pallas_call(functools.partial(sketch_kernel, n_rows, n_cols), out_shap...]
    reduce_scatter x2 -> x0, waiting for transfers between devices: 133 us -> none  [the longest x1 87.7 us: per_device(): lax.psum_scatter(partial_p, 'rows', scatter_dimension=0, tiled=True)]
    psum x1 -> x0, waiting for transfers between devices: 127 us -> none  [per_device(): gram_total = lax.psum(gram, ('rows', 'cols'))]
    another operation x17 -> x0, other arithmetic: 122 us -> none  [the longest x14 79.2 us: basis_map(): lower = jnp.linalg.cholesky(gram_total)]
    another operation x17 -> x0, local copies, waits for them, and re-layouts: 14.5 us -> none
    pallas_call x1, Pallas kernels: 29.8 us -> 17 us  [dense_tiles(): pl.pallas_call(tiles_kernel, out_shape=jax.ShapeDtypeStruct((col_blocks,...]
    another operation x13 -> x0, matrix products: 12.3 us -> none  [the longest x7 6.83 us: basis_map(): inverse = jax.scipy.linalg.solve_triangular(lower, identity, lower=True)]
    convert_element_type x0 -> x2, local copies, waits for them, and re-layouts: none -> 6.73 us  [per_device(): projected = project_scatter(partial_p.astype(jnp.bfloat16))]
  transfers between devices with their start and end apart: 4 -> 1, of which waited for: 4 -> 1; matrix products, arithmetic and copies ran while one was open for 0% -> 0% of each run, Pallas kernels for 0% -> 0%
where the time goes in v2:
time: 251 us; the launch traced here: 253 us
  Pallas kernels  182 us (73%)
  waiting for transfers between devices  23.3 us (9%)
  matrix products  17.3 us (7%)
  between operations  14.9 us (6%)
  local copies, waits for them, and re-layouts  13.5 us (5%)
    pallas_call x1, Pallas kernels, sketch_and_gram(): pl.pallas_call(functools.partial(sketch_kernel, n_rows, n_cols), out_shap...  79.4 us
    pallas_call x1, Pallas kernels, project_scatter(): pl.pallas_call(functools.partial(project_kernel, n_rows), out_shape=jax.S...  49.6 us
    pallas_call x1, Pallas kernels, lower_inverse(): pl.pallas_call(inverse_kernel, out_shape=jax.ShapeDtypeStruct((size, size...  35.9 us
    all_gather x1, waiting for transfers between devices, per_device(): lax.all_gather(share_q.astype(jnp.bfloat16), 'cols', axis=0, tiled=True)  23.3 us
    pallas_call x1, Pallas kernels, dense_tiles(): pl.pallas_call(tiles_kernel, out_shape=jax.ShapeDtypeStruct((col_blocks,...  17 us
    dot_general x1, matrix products, per_device(): lax.dot_general(q_round, matrix, (((0,), (1,)), ((), ())), preferred_elem...  8.57 us
    convert_element_type x2, local copies, waits for them, and re-layouts, per_device(): projected = project_scatter(partial_p.astype(jnp.bfloat16))  6.73 us
    dot_general x1, matrix products, per_device(): lax.dot_general(matrix, gauss_sketch.reshape(col_blocks, TILE, samples),...  5.95 us
  transfers between devices with their start and end apart: 1, of which 1 were waited for; matrix products, arithmetic and copies ran while one was open for 0% of the time, Pallas kernels for 0%

profile of v2, /device:TPU:11, one launch (start us, length us, event | category | flops | bytes accessed | tf_op | source)
XLA Modules:
  0.0 252.7 jit_solution(12982005424379191390)
XLA Ops:
  7.2 0.0 copy-start
  7.2 0.0 all-gather.2.cloned.1.call-start
  8.0 0.8 copy.24
  8.8 0.8 pad_maximum_fusion
  9.6 0.4 copy.26
  9.9 0.1 pad_add_fusion
  10.0 0.8 maximum_bitcast_fusion.walls_ref
  10.8 17.0 %shard_map.86 = bf16[8,2048,256]{2,1,0:T(8,128)(2,1)S(1)} custom-call(s32[48,2]{1,0:T(8,128)S(1)} %broadcast_subtract_fusion.list_ref, s32[1]{0:T(128)} %bitcast.31.count_ref, f32[2048,4]{1,0:T(8,128)S(1)} %bitcast.34, f32[8,4,256]{2,1,0:T(4,128)S(1)} %maximum_bitcast_fusion.walls_ref), custom_call_target="tpu_custom_call" | custom-call | tf_op jit(solution)/shard_map/pallas_call | solution.py:79
  27.8 0.0 copy-done
  27.9 0.0 copy-start.2
  27.9 3.2 %copy-done.2 = bf16[8,2048,256]{2,1,0:T(8,128)(2,1)} copy-done((bf16[8,2048,256]{2,1,0:T(8,128)(2,1)}, bf16[8,2048,256]{2,1,0:T(8,128)(2,1)S(1)}, u32[]{:S(2)}) %copy-start.2) | copy-done | bytes 8388632
  31.1 6.0 %convolution_bitcast_fusion.y_ref = f32[4,512,512]{2,1,0:T(8,128)} fusion(bf16[4,512,8,256]{3,1,0,2:T(8,128)(2,1)S(1)} %bitcast.33, bf16[8,256,512,1]{2,1,3,0:T(8,128)(2,1)S(1)} %bitcast.32), kind=kOutput, calls=%fused_computation | convolution fusion | flops 4294967296 | bytes 14680064 | tf_op jit(solution)/shard_map/dot_general | solution.py:417
  37.0 79.4 %shard_map.87 = (f32[512,512]{1,0:T(8,128)S(1)}, f32[4,8,16,512]{3,2,1,0:T(8,128)S(1)}) custom-call(f32[4,512,512]{2,1,0:T(8,128)} %convolution_bitcast_fusion.y_ref), custom_call_target="tpu_custom_call" | custom-call | tf_op jit(solution)/shard_map/pallas_call | solution.py:328
  116.5 35.9 %shard_map.88 = f32[512,512]{1,0:T(8,128)S(1)} custom-call(f32[512,512]{1,0:T(8,128)S(1)} %bitcast.35), custom_call_target="tpu_custom_call" | custom-call | tf_op jit(solution)/shard_map/pallas_call | solution.py:172
  152.4 2.8 %fusion.5 = (bf16[512,512]{1,0:T(8,128)(2,1)}, bf16[512,512]{1,0:T(8,128)(2,1)}) fusion(f32[512,512]{1,0:T(8,128)S(1)} %get-tuple-element.4, f32[512,512]{1,0:T(8,128)S(1)} %shard_map.88), kind=kOutput, calls=%fused_computation.9 | convolution fusion | flops 1611399168 | bytes 3145728 | tf_op jit(solution)/shard_map/dot_general | solution.py:93
  155.3 0.0 all-gather.2.cloned.1.call-update
  155.3 23.3 %all-gather.2.cloned.1.call-done = bf16[2048,512]{1,0:T(8,128)(2,1)} async-done(((bf16[512,512]{1,0:T(8,128)(2,1)}), bf16[2048,512]{1,0:T(8,128)(2,1)}) %all-gather.2.cloned.1.call-update) | async-done | bytes 2097168 | tf_op jit(solution)/shard_map/all_gather | solution.py:427
  178.5 8.6 %fusion.2 = bf16[512,8,256]{2,0,1:T(8,128)(2,1)S(1)} fusion(bf16[8,2048,256]{2,1,0:T(8,128)(2,1)} %copy-done.2, bf16[2048,512]{1,0:T(8,128)(2,1)} %all-gather.2.cloned.1.call-done), kind=kOutput, calls=%fused_computation.3 | convolution fusion | flops 4296015872 | bytes 12582912 | tf_op jit(solution)/shard_map/dot_general | solution.py:428
  187.1 2.5 %copy.28 = bf16[512,8,256]{2,1,0:T(8,128)(2,1)} copy(bf16[512,8,256]{2,0,1:T(8,128)(2,1)S(1)} %fusion.2) | data formatting | bytes 4194304 | tf_op jit(solution)/shard_map/convert_element_type | solution.py:431
  189.7 4.2 %convert_element_type.16.p_ref = bf16[8,64,2048]{2,1,0:T(8,128)(2,1)} reshape(bf16[512,8,256]{2,1,0:T(8,128)(2,1)} %copy.28) | data formatting | bytes 4194304 | tf_op jit(solution)/shard_map/convert_element_type | solution.py:431
  193.8 0.0 copy-start.1
  193.8 1.6 copy-done.1
  195.4 49.6 %shard_map.89 = f32[64,2048]{1,0:T(8,128)S(1)} custom-call(bf16[8,64,2048]{2,1,0:T(8,128)(2,1)S(1)} %copy-done.1), custom_call_target="tpu_custom_call" | custom-call | tf_op jit(solution)/shard_map/pallas_call | solution.py:382
  245.1 0.8 copy.34
  (1 shorter events, 0.0 us)
Async XLA Ops:
  7.2 20.7 %copy-start = (bf16[2048,512]{1,0:T(8,128)(2,1)S(1)}, bf16[2048,512]{1,0:T(8,128)(2,1)}, u32[]{:S(2)}) copy-start(bf16[2048,512]{1,0:T(8,128)(2,1)} %param.11) | copy-start | bytes 6291460
  7.2 171.4 %all-gather.2.cloned.1.call-start = ((), (), s32[]{:S(2)}) async-start(), calls=%async_computation | async-start | bytes 2621440 | tf_op jit(solution)/shard_map/all_gather | solution.py:427
  27.9 3.2 %copy-start.2 = (bf16[8,2048,256]{2,1,0:T(8,128)(2,1)}, bf16[8,2048,256]{2,1,0:T(8,128)(2,1)S(1)}, u32[]{:S(2)}) copy-start(bf16[8,2048,256]{2,1,0:T(8,128)(2,1)S(1)} %shard_map.86) | copy-start | bytes 25165828
  193.8 1.6 copy-start.1
Sparse Core Ops, SparseCore 0:
  155.4 23.0 all-gather.1

commit v3 on v2

--- a/solution.py
+++ b/solution.py
@@ -207,6 +207,36 @@
 def wait_all(copies):
     for copy in copies:
         copy.wait()
+
+
+def toggled(index, mask):
+    bit = 1
+    while bit <= mask:
+        if mask & bit:
+            index = index + bit * (1 - 2 * ((index // bit) % 2))
+        bit *= 2
+    return index
+
+
+def tree_gather(n_cols, shares, send_sem, recv_sem, use):
+    me_row = lax.axis_index("rows")
+    me_col = lax.axis_index("cols")
+    copies = {}
+    for mask in range(n_cols):
+        if mask:
+            copies[mask].wait()
+        slot = toggled(me_col, mask)
+        bit = 1
+        while bit < (mask & -mask if mask else n_cols):
+            copies[mask | bit] = send(
+                shares.at[slot],
+                shares.at[slot],
+                send_sem.at[(mask | bit) - 1],
+                recv_sem.at[(mask | bit) - 1],
+                (me_row, toggled(me_col, bit)),
+            )
+            bit *= 2
+        use(mask, slot)
 
 
 def sketch_kernel(
@@ -307,12 +337,7 @@
         for d, peer in enumerate(row_peers)
     ]
     wait_all(copies)
-    mine = whole.at[me_col]
-    copies = [
-        send(mine, mine, col_send.at[1, d], col_recv.at[1, d], peer)
-        for d, peer in enumerate(col_peers)
-    ]
-    wait_all(copies)
+    tree_gather(n_cols, whole, col_send.at[1], col_recv.at[1], lambda mask, slot: None)
     gram_ref[...] = whole[...]
 
 
@@ -359,40 +384,116 @@
     return share_y, gram.reshape(samples, samples)
 
 
-def project_kernel(n_rows, p_ref, out_ref, arrived, send_sem, recv_sem):
+def finish_kernel(
+    n_rows,
+    n_cols,
+    basis_scale,
+    share_ref,
+    inverse_ref,
+    matrix_ref,
+    basis_ref,
+    out_ref,
+    matrix,
+    shares,
+    total,
+    leaving,
+    arrived,
+    load_sem,
+    gather_send,
+    gather_recv,
+    send_sem,
+    recv_sem,
+):
     me_row = lax.axis_index("rows")
     me_col = lax.axis_index("cols")
-    peers = [(lax.rem(me_row + d, n_rows), me_col) for d in range(1, n_rows)]
-    greet(peers)
-    copies = [
-        send(p_ref.at[peer[0]], arrived.at[d], send_sem.at[d], recv_sem.at[d], peer)
-        for d, peer in enumerate(peers)
-    ]
-    out_ref[...] = p_ref[me_row].astype(jnp.float32)
-    for d, copy in enumerate(copies):
-        copy.wait()
-        out_ref[...] += arrived[d].astype(jnp.float32)
-
-
-def project_scatter(partial_p):
-    n_rows = lax.axis_size("rows")
-    samples, wall_cells = partial_p.shape
+    row_peers = [(lax.rem(me_row + d, n_rows), me_col) for d in range(1, n_rows)]
+    col_peers = [(me_row, lax.rem(me_col + d, n_cols)) for d in range(1, n_cols)]
+    load = pltpu.make_async_copy(matrix_ref, matrix, load_sem)
+    load.start()
+    greet(row_peers + col_peers)
+    share_rows = share_ref.shape[0]
+    col_blocks, _, tile = matrix.shape
+    groups, _, part, width = leaving.shape
+    share_q = full_dot(share_ref[...], inverse_ref[...], 1, 1)
+    shares[me_col] = share_q.T.astype(jnp.bfloat16)
+    basis_ref[...] = (basis_scale * share_q).astype(jnp.bfloat16)
+    copies = []
+
+    def product(slot, block):
+        rows = pl.ds(pl.multiple_of(slot * share_rows, share_rows), share_rows)
+        return jnp.dot(
+            shares[slot], matrix[block, rows, :], preferred_element_type=jnp.float32
+        )
+
+    def use(mask, slot):
+        if mask == 0:
+            load.wait()
+        for block in range(col_blocks):
+            value = product(slot, block)
+            if mask:
+                value = value + total[block]
+            if mask < n_cols - 1:
+                total[block] = value
+                continue
+            group, place = divmod(block * tile, width)
+            leaving[group, :, :, place : place + tile] = value.reshape(
+                n_rows, part, tile
+            ).astype(jnp.bfloat16)
+            if place + tile == width:
+                for d, peer in enumerate(row_peers):
+                    copies.append(
+                        send(
+                            leaving.at[group, peer[0]],
+                            arrived.at[d, group],
+                            send_sem.at[d, group],
+                            recv_sem.at[d, group],
+                            peer,
+                        )
+                    )
+
+    tree_gather(n_cols, shares, gather_send, gather_recv, use)
+    wait_all(copies)
+    for group in range(groups):
+        value = leaving[group, me_row].astype(jnp.float32)
+        for d in range(n_rows - 1):
+            value = value + arrived[d, group].astype(jnp.float32)
+        out_ref[:, group * width : (group + 1) * width] = value
+
+
+def finish(share_y, inverse, matrix, basis_scale):
+    n_rows, n_cols = lax.axis_size("rows"), lax.axis_size("cols")
+    share_rows, samples = share_y.shape
+    col_blocks, local_rows, tile = matrix.shape
+    wall_cells = col_blocks * tile
     part = samples // n_rows
+    groups = 2
+    width = wall_cells // groups
     vmem = pl.BlockSpec(memory_space=pltpu.VMEM)
+    dma = pltpu.SemaphoreType.DMA
     return pl.pallas_call(
-        functools.partial(project_kernel, n_rows),
-        out_shape=jax.ShapeDtypeStruct((part, wall_cells), jnp.float32),
-        in_specs=[vmem],
-        out_specs=vmem,
+        functools.partial(finish_kernel, n_rows, n_cols, basis_scale),
+        out_shape=(
+            jax.ShapeDtypeStruct((share_rows, samples), jnp.bfloat16),
+            jax.ShapeDtypeStruct((part, wall_cells), jnp.float32),
+        ),
+        in_specs=[vmem, vmem, pl.BlockSpec(memory_space=pl.ANY)],
+        out_specs=(vmem, vmem),
         scratch_shapes=[
-            pltpu.VMEM((n_rows - 1, part, wall_cells), jnp.bfloat16),
-            pltpu.SemaphoreType.DMA((n_rows - 1,)),
-            pltpu.SemaphoreType.DMA((n_rows - 1,)),
+            pltpu.VMEM(matrix.shape, jnp.bfloat16),
+            pltpu.VMEM((n_cols, samples, share_rows), jnp.bfloat16),
+            pltpu.VMEM((col_blocks, samples, tile), jnp.float32),
+            pltpu.VMEM((groups, n_rows, part, width), jnp.bfloat16),
+            pltpu.VMEM((n_rows - 1, groups, part, width), jnp.bfloat16),
+            dma,
+            dma((n_cols - 1,)),
+            dma((n_cols - 1,)),
+            dma((n_rows - 1, groups)),
+            dma((n_rows - 1, groups)),
         ],
         compiler_params=pltpu.CompilerParams(
-            collective_id=1, has_side_effects=True, vmem_limit_bytes=32 * 2**20
+            collective_id=1, has_side_effects=True, vmem_limit_bytes=48 * 2**20
         ),
-    )(partial_p.reshape(n_rows, part, wall_cells))
+    )(share_y, inverse, matrix)
 
 
 def per_device(
@@ -422,14 +523,7 @@
     )
     basis_scale = math.sqrt(local_rows * lax.axis_size("rows"))
     share_y, gram_total = sketch_and_gram(partial_y)
-    share_q = full_dot(share_y, lower_inverse(gram_total), 1, 1)
-    basis_out = (basis_scale * share_q).astype(jnp.bfloat16)
-    q_round = lax.all_gather(share_q.astype(jnp.bfloat16), "cols", axis=0, tiled=True)
-    partial_p = lax.dot_general(
-        q_round, matrix, (((0,), (1,)), ((), ())), preferred_element_type=jnp.float32
-    ).reshape(samples, wall_cells)
-    projected = project_scatter(partial_p.astype(jnp.bfloat16))
-    return (basis_out, projected)
+    return finish(share_y, lower_inverse(gram_total), matrix, basis_scale)
 
 
 def solution(mesh):

time: 251 us -> 208 us (0.83); the launches traced: 253 us -> 206 us
  waiting for transfers between devices: 23.3 us -> 0 us
  between operations: 14.9 us -> 1.49 us
  Pallas kernels: 182 us -> 194 us
  matrix products: 17.3 us -> 5.95 us
  local copies, waits for them, and re-layouts: 13.5 us -> 3.44 us
    all_gather x1 -> x0, waiting for transfers between devices: 23.3 us -> none  [per_device(): lax.all_gather(share_q.astype(jnp.bfloat16), 'cols', axis=0, tiled=True)]
    pallas_call x1, Pallas kernels: 49.6 us -> 66.2 us  [finish(): pl.pallas_call(functools.partial(finish_kernel, n_rows, n_cols, basis_sca...]
    pallas_call x1, Pallas kernels: 79.4 us -> 63.6 us  [sketch_and_gram(): pl.pallas_call(functools.partial(sketch_kernel, n_rows, n_cols), out_shap...]
    dot_general x2 -> x0, matrix products: 11.4 us -> none  [the longest x1 8.57 us: per_device(): lax.dot_general(q_round, matrix, (((0,), (1,)), ((), ())), preferred_elem...]
    pallas_call x1, Pallas kernels: 17 us -> 27.8 us  [dense_tiles(): pl.pallas_call(tiles_kernel, out_shape=jax.ShapeDtypeStruct((col_blocks,...]
    convert_element_type x2 -> x0, local copies, waits for them, and re-layouts: 6.73 us -> none  [per_device(): projected = project_scatter(partial_p.astype(jnp.bfloat16))]
    unnamed x7 -> x6, local copies, waits for them, and re-layouts: 5.63 us -> 2.32 us
  transfers between devices with their start and end apart: 1 -> 0, of which waited for: 1 -> 0; matrix products, arithmetic and copies ran while one was open for 0% -> 0% of each run, Pallas kernels for 0% -> 0%
where the time goes in v3:
time: 208 us; the launch traced here: 206 us
  Pallas kernels  194 us (93%)
  matrix products  5.95 us (3%)
  local copies, waits for them, and re-layouts  3.44 us (2%)
    pallas_call x1, Pallas kernels, finish(): pl.pallas_call(functools.partial(finish_kernel, n_rows, n_cols, basis_sca...  66.2 us
    pallas_call x1, Pallas kernels, sketch_and_gram(): pl.pallas_call(functools.partial(sketch_kernel, n_rows, n_cols), out_shap...  63.6 us
    pallas_call x1, Pallas kernels, lower_inverse(): pl.pallas_call(inverse_kernel, out_shape=jax.ShapeDtypeStruct((size, size...  36 us
    pallas_call x1, Pallas kernels, dense_tiles(): pl.pallas_call(tiles_kernel, out_shape=jax.ShapeDtypeStruct((col_blocks,...  27.8 us
    dot_general x1, matrix products, per_device(): lax.dot_general(matrix, gauss_sketch.reshape(col_blocks, TILE, samples),...  5.95 us

profile of v3, /device:TPU:11, one launch (start us, length us, event | category | flops | bytes accessed | tf_op | source)
XLA Modules:
  0.0 206.1 jit_solution(3370569221652768924)
XLA Ops:
  0.6 0.0 copy-start
  1.4 0.1 pad_add_fusion
  1.5 0.7 copy-done
  2.2 0.8 copy.18
  3.0 0.8 pad_maximum_fusion
  3.8 0.8 maximum_bitcast_fusion.walls_ref
  4.6 0.4 copy.20
  5.0 27.8 %shard_map.86.matrix_ref = bf16[8,2048,256]{2,1,0:T(8,128)(2,1)S(1)} custom-call(s32[48,2]{1,0:T(8,128)S(1)} %broadcast_subtract_fusion.list_ref, s32[1]{0:T(128)} %bitcast.23.count_ref, f32[2048,4]{1,0:T(8,128)S(1)} %bitcast.26, f32[8,4,256]{2,1,0:T(4,128)S(1)} %maximum_bitcast_fusion.walls_ref), custom_call_target="tpu_custom_call" | custom-call | tf_op jit(solution)/shard_map/pallas_call | solution.py:79
  32.8 0.0 copy-start.1
  32.8 5.9 %convolution_bitcast_fusion.y_ref = f32[4,512,512]{2,1,0:T(8,128)} fusion(bf16[4,512,8,256]{3,1,0,2:T(8,128)(2,1)S(1)} %bitcast.25, bf16[8,256,512,1]{2,1,3,0:T(8,128)(2,1)S(1)} %bitcast.24), kind=kOutput, calls=%fused_computation | convolution fusion | flops 4294967296 | bytes 14680064 | tf_op jit(solution)/shard_map/dot_general | solution.py:518
  38.8 0.0 copy-done.1
  38.8 63.6 %shard_map.87 = (f32[512,512]{1,0:T(8,128)S(1)}, f32[4,8,16,512]{3,2,1,0:T(8,128)S(1)}) custom-call(f32[4,512,512]{2,1,0:T(8,128)} %convolution_bitcast_fusion.y_ref), custom_call_target="tpu_custom_call" | custom-call | tf_op jit(solution)/shard_map/pallas_call | solution.py:353
  102.4 36.0 %shard_map.88.inverse_ref = f32[512,512]{1,0:T(8,128)S(1)} custom-call(f32[512,512]{1,0:T(8,128)S(1)} %bitcast.27), custom_call_target="tpu_custom_call" | custom-call | tf_op jit(solution)/shard_map/pallas_call | solution.py:172
  138.3 66.2 %shard_map.89 = (bf16[512,512]{1,0:T(8,128)(2,1)S(1)}, f32[64,2048]{1,0:T(8,128)S(1)}) custom-call(f32[512,512]{1,0:T(8,128)S(1)} %get-tuple-element.4.share_ref, f32[512,512]{1,0:T(8,128)S(1)} %shard_map.88.inverse_ref, bf16[8,2048,256]{2,1,0:T(8,128)(2,1)} %copy-done.1), custom_call_target="tpu_custom_call" | custom-call | tf_op jit(solution)/shard_map/pallas_call | solution.py:473
  204.6 0.8 copy.25
  205.4 0.8 copy.26
  (1 shorter events, 0.0 us)
Async XLA Ops:
  0.6 1.6 copy-start
  32.8 6.0 %copy-start.1 = (bf16[8,2048,256]{2,1,0:T(8,128)(2,1)}, bf16[8,2048,256]{2,1,0:T(8,128)(2,1)S(1)}, u32[]{:S(2)}) copy-start(bf16[8,2048,256]{2,1,0:T(8,128)(2,1)S(1)} %shard_map.86.matrix_ref) | copy-start | bytes 25165828
